TPU v7x, 32 devices: a whole 2x2x4 slice. The times are simulated.
32 devices in a mesh: ch: 16 (over z, x, core), ta: 2 (over y).
Axes of the slice: x: 2, y: 2, z: 4, core: 2. Of those that a mesh axis runs over, the one named last changes fastest.
Arguments:
- raw_strain: float32 [2048, 3072], P('ch', 'ta'), may hold values from -6 to 6
- band_index: int32 [2048], P('ch'), may hold values from 0 to 3
- filter_taps: float32 [4, 33], replicated, may hold values from -1 to 1
Outputs:
- correlation: float32 [2, 65, 2048, 128], P(None, None, ('ch', 'ta'))
All inputs are finite; a program needn't handle non-finite values.
Results may differ from a plain program's by a relative error of at most 0.0037.
Values may be sent and summed in bfloat16 or wider, within the bound.
A program may use at most 64 MiB of HBM per device.

v0:
```python
import math

import jax
import jax.numpy as jnp
from jax import lax
from jax.sharding import PartitionSpec as P

HF = 16
TAPS = 33
NBANDS = 4
LAGH = 32
LAGS = 65
ROUNDS = 2


def padded_2(block, sides, width):
    for axis, dim in sides:
        count = lax.axis_size(axis)
        forward = [(i, i + 1) for i in range(count - 1)]
        backward = [(target, source) for source, target in forward]
        low = lax.ppermute(
            lax.slice_in_dim(block, block.shape[dim] - width, None, axis=dim), axis, forward
        )
        high = lax.ppermute(lax.slice_in_dim(block, 0, width, axis=dim), axis, backward)
        block = jnp.concatenate([low, block, high], axis=dim)
    return block


def passed_along(block, axis, distance):
    devices = range(lax.axis_size(axis))
    route = [((i - distance) % len(devices), i) for i in devices]
    return lax.ppermute(block, axis, route)


def correlate(own_rows, partner, scale):
    row_count = own_rows.shape[0]
    length = own_rows.shape[1]
    padded = jnp.pad(own_rows, ((0, 0), (LAGH, LAGH)))

    def lag_block(carry, block_id):
        pieces = []
        for inner in range(5):
            start = 2 * LAGH - (block_id * 5 + inner)
            pieces.append(lax.dynamic_slice_in_dim(padded, start, length, 1))
        stacked = jnp.concatenate(pieces, axis=0)
        result = lax.dot_general(
            stacked, partner, (((1,), (1,)), ((), ())), preferred_element_type=jnp.float32
        )
        return (carry, result.reshape(5, row_count, partner.shape[0]) * scale)

    unused, lagged = lax.scan(lag_block, 0, jnp.arange(LAGS // 5, dtype=jnp.int32))
    return lagged.reshape(LAGS, row_count, partner.shape[0])


def on_device(raw_strain, band_index, filter_taps):
    block_size = raw_strain.shape[0]
    local_len = raw_strain.shape[1]
    time_groups = lax.axis_size("ta")
    channel_groups = lax.axis_size("ch")
    whole_len = local_len * time_groups
    onehot = (band_index[:, None] == jnp.arange(NBANDS, dtype=jnp.int32)[None, :]).astype(
        jnp.float32
    )
    coeffs = jnp.dot(
        onehot, filter_taps, precision=lax.Precision.HIGHEST, preferred_element_type=jnp.float32
    )
    extended = padded_2(raw_strain, (("ta", 1),), HF)
    filtered = jnp.zeros_like(raw_strain)
    for step in range(TAPS):
        filtered = filtered + coeffs[:, step : step + 1] * extended[:, step : step + local_len]
    magnitude = padded_2(jnp.abs(filtered), (("ta", 1),), local_len)
    cumulative = jnp.concatenate(
        [jnp.zeros((block_size, 1), jnp.float32), jnp.cumsum(magnitude, axis=1)], axis=1
    )
    window_sum = cumulative[:, 2 * local_len + 1 : 3 * local_len + 1] - cumulative[:, 0:local_len]
    global_time = lax.axis_index("ta") * local_len + jnp.arange(local_len, dtype=jnp.int32)
    upper = jnp.minimum(global_time + local_len, whole_len - 1) + 1
    lower = jnp.maximum(global_time - local_len, 0)
    counted = (upper - lower).astype(jnp.float32)
    level = window_sum / counted[None, :]
    normalized = (filtered / (level + 1e-06)).astype(jnp.bfloat16)
    row_count = block_size // time_groups
    scale = 1.0 / math.sqrt(whole_len)
    results = []
    own_whole = lax.all_gather(normalized, "ta", axis=1, tiled=True)
    own_part = lax.dynamic_slice_in_dim(own_whole, lax.axis_index("ta") * row_count, row_count, 0)
    for round_id in range(ROUNDS):
        offset = (round_id + 1) * (channel_groups // 4)
        partner = passed_along(own_whole, "ch", offset)
        results.append(correlate(own_part, partner, scale))
    return jnp.stack(results)


def solution(mesh):
    placed = (P("ch", "ta"), P("ch"), P())
    return jax.shard_map(
        on_device,
        mesh=mesh,
        in_specs=placed,
        out_specs=P(None, None, ("ch", "ta"), None),
        check_vma=False,
    )
```

profile of v0, /device:TPU:18, one launch (start us, length us, event | category | flops | bytes accessed | tf_op | source)
XLA Modules:
  0.0 189.7 jit_solution(6716087059136399076)
XLA Ops:
  0.0 1.4 copy.5
  1.4 3.4 %collective-permute-start = (f32[128,16]{0,1:T(8,128)S(1)}, f32[128,16]{0,1:T(8,128)S(1)}, u32[]{:S(2)}, u32[]{:S(2)}) collective-permute-start(f32[128,16]{0,1:T(8,128)S(1)} %get-tuple-element.207), channel_id=1, source_target_pairs={{0,1},{2,3},{4,5},{6,7},{8,9},{10,11},{12,13},{14,15},{16,17},{18,... | collective-permute-start | bytes 24584 | tf_op jit(solution)/shard_map/ppermute | solution.py:21
  4.9 1.3 collective-permute-start.1
  6.2 0.9 fusion.101
  7.2 3.2 %collective-permute-done.1 = f32[128,16]{0,1:T(8,128)S(1)} collective-permute-done((f32[128,16]{0,1:T(8,128)S(1)}, f32[128,16]{0,1:T(8,128)S(1)}, u32[]{:S(2)}, u32[]{:S(2)}) %collective-permute-start.1) | collective-permute-done | bytes 8224 | tf_op jit(solution)/shard_map/ppermute | solution.py:24
  10.4 4.7 %fusion.103 = (f32[128,1536]{0,1:T(8,128)S(1)}, f32[128,1536]{0,1:T(8,128)S(1)}) fusion(f32[128,16]{0,1:T(8,128)S(1)} %collective-permute-done.1, f32[128,1536]{0,1:T(8,128)S(1)} %copy.5, f32[128]{0:T(128)S(1)} %get-tuple-element.210, f32[128]{0:T(128)S(1)} %get-tuple-element.211, f32[128]{0:T(128)S(1)} %get-tuple-element.212, ...), kind=kLoop, calls=%fused_computation.212 | loop fusion | flops 19267584 | bytes 2392576 | tf_op jit(solution)/shard_map/abs | solution.py:71
  15.1 1.7 collective-permute-start.2
  16.8 1.3 collective-permute-start.3
  18.2 14.6 %collective-permute-done.2 = f32[128,1536]{0,1:T(8,128)S(1)} collective-permute-done((f32[128,1536]{0,1:T(8,128)S(1)}, f32[128,1536]{0,1:T(8,128)S(1)}, u32[]{:S(2)}, u32[]{:S(2)}) %collective-permute-start.2) | collective-permute-done | bytes 786464 | tf_op jit(solution)/shard_map/ppermute | solution.py:21
  32.8 4.2 %collective-permute-done.3 = f32[128,1536]{0,1:T(8,128)S(1)} collective-permute-done((f32[128,1536]{0,1:T(8,128)S(1)}, f32[128,1536]{0,1:T(8,128)S(1)}, u32[]{:S(2)}, u32[]{:S(2)}) %collective-permute-start.3) | collective-permute-done | bytes 786464 | tf_op jit(solution)/shard_map/ppermute | solution.py:24
  37.1 1.4 fusion
  39.5 9.6 %all_gather.3 = bf16[128,3072]{0,1:T(8,128)(2,1)} all-gather(bf16[128,1536]{0,1:T(8,128)(2,1)S(1)} %fusion.100), channel_id=1, replica_groups=mesh['ch'=16,'ta'=2] {'ta'}, dimensions={1}, use_global_device_ids=true | all-gather | bytes 1179648 | tf_op jit(solution)/shard_map/all_gather | solution.py:85
  49.1 1.6 collective-permute-start.4
  51.0 1.4 constant_dynamic-slice_fusion
  52.9 33.7 %collective-permute-done.4 = bf16[128,3072]{0,1:T(8,128)(2,1)S(1)} collective-permute-done((bf16[128,3072]{0,1:T(8,128)(2,1)}, bf16[128,3072]{0,1:T(8,128)(2,1)S(1)}, u32[]{:S(2)}, u32[]{:S(2)}) %collective-permute-start.4) | collective-permute-done | bytes 786464 | tf_op jit(solution)/shard_map/ppermute | solution.py:32
  87.0 1.6 broadcast.74.clone.1
  88.6 47.8 %while.26 = (s32[]{:T(128)}, f32[13,5,64,128]{3,2,1,0:T(8,128)}, s32[13]{0:T(128)S(1)}, bf16[64,3136]{1,0:T(8,128)(2,1)S(1)}, bf16[128,3072]{1,0:T(8,128)(2,1)S(...) while((s32[]{:T(128)}, f32[13,5,64,128]{3,2,1,0:T(8,128)}, ...), condition=%wide.region_3.4_spmd, body=%wide.region_2.3_spmd.sunk | while | flops 251699232 | bytes 7177159 | solution.py:51
  95.2 0.7 constant_dynamic-update-slice_fusion.4
  136.4 1.4 copy.15
  137.8 1.6 broadcast.74.clone
  139.4 45.4 %while.27 = (s32[]{:T(128)}, f32[13,5,64,128]{3,2,1,0:T(8,128)}, s32[13]{0:T(128)S(1)}, bf16[64,3136]{1,0:T(8,128)(2,1)S(1)}, bf16[128,3072]{1,0:T(8,128)(2,1)S(...) while((s32[]{:T(128)}, f32[13,5,64,128]{3,2,1,0:T(8,128)}, ...), condition=%wide.region_5.6_spmd, body=%wide.region_4.5_spmd.sunk | while | flops 251699232 | bytes 7177159 | solution.py:51
  152.7 0.7 constant_dynamic-update-slice_fusion.5
  166.7 0.7 constant_dynamic-update-slice_fusion.5
  184.8 4.9 %pad_maximum_fusion = f32[2,65,64,128]{3,2,1,0:T(8,128)} fusion(f32[1,65,64,128]{3,2,1,0:T(8,128)} %bitcast.59, f32[1,65,64,128]{3,2,1,0:T(8,128)} %bitcast.58), kind=kLoop, calls=%fused_computation.44 | loop fusion | flops 1064960 | bytes 8519680 | tf_op jit(solution)/shard_map/stack | solution.py:91
  (225 shorter events, 75.1 us)
Async XLA Ops:
  0.0 6.2 %copy-start = (f32[4,33]{1,0:T(4,128)S(1)}, f32[4,33]{1,0:T(4,128)}, u32[]{:S(2)}) copy-start(f32[4,33]{1,0:T(4,128)} %param.9) | copy-start | bytes 1588
  1.4 5.7 %collective-permute-start = (f32[128,16]{0,1:T(8,128)S(1)}, f32[128,16]{0,1:T(8,128)S(1)}, u32[]{:S(2)}, u32[]{:S(2)}) collective-permute-start(f32[128,16]{0,1:T(8,128)S(1)} %get-tuple-element.207), channel_id=1, source_target_pairs={{0,1},{2,3},{4,5},{6,7},{8,9},{10,11},{12,13},{14,15},{16,17},{18,... | collective-permute-start | bytes 24584 | tf_op jit(solution)/shard_map/ppermute | solution.py:21
  4.9 5.5 %collective-permute-start.1 = (f32[128,16]{0,1:T(8,128)S(1)}, f32[128,16]{0,1:T(8,128)S(1)}, u32[]{:S(2)}, u32[]{:S(2)}) collective-permute-start(f32[128,16]{0,1:T(8,128)S(1)} %get-tuple-element.208), channel_id=1, source_target_pairs={{1,0},{3,2},{5,4},{7,6},{9,8},{11,10},{13,12},{15,14},{17,16},{19,... | collective-permute-start | bytes 24584 | tf_op jit(solution)/shard_map/ppermute | solution.py:24
  15.1 17.6 %collective-permute-start.2 = (f32[128,1536]{0,1:T(8,128)S(1)}, f32[128,1536]{0,1:T(8,128)S(1)}, u32[]{:S(2)}, u32[]{:S(2)}) collective-permute-start(f32[128,1536]{0,1:T(8,128)S(1)} %get-tuple-element.205), channel_id=1, source_target_pairs={{0,1},{2,3},{4,5},{6,7},{8,9},{10,11},{12,13},{14,15},{16,17},{18,... | collective-permute-start | bytes 2359304 | tf_op jit(solution)/shard_map/ppermute | solution.py:21
  16.8 20.1 %collective-permute-start.3 = (f32[128,1536]{0,1:T(8,128)S(1)}, f32[128,1536]{0,1:T(8,128)S(1)}, u32[]{:S(2)}, u32[]{:S(2)}) collective-permute-start(f32[128,1536]{0,1:T(8,128)S(1)} %get-tuple-element.205), channel_id=1, source_target_pairs={{1,0},{3,2},{5,4},{7,6},{9,8},{11,10},{13,12},{15,14},{17,16},{19,... | collective-permute-start | bytes 2359304 | tf_op jit(solution)/shard_map/ppermute | solution.py:24
  49.1 37.5 %collective-permute-start.4 = (bf16[128,3072]{0,1:T(8,128)(2,1)}, bf16[128,3072]{0,1:T(8,128)(2,1)S(1)}, u32[]{:S(2)}, u32[]{:S(2)}) collective-permute-start(bf16[128,3072]{0,1:T(8,128)(2,1)} %all_gather.3), channel_id=1, source_target_pairs={{24,0},{26,2},{28,4},{30,6},{0,8},{2,10},{4,12},{6,14},{8,16},{10,... | collective-permute-start | bytes 2359304 | tf_op jit(solution)/shard_map/ppermute | solution.py:32
  50.7 85.7 %collective-permute-start.5 = (bf16[128,3072]{0,1:T(8,128)(2,1)}, bf16[128,3072]{0,1:T(8,128)(2,1)}, u32[]{:S(2)}, u32[]{:S(2)}) collective-permute-start(bf16[128,3072]{0,1:T(8,128)(2,1)} %all_gather.3), channel_id=1, source_target_pairs={{16,0},{18,2},{20,4},{22,6},{24,8},{26,10},{28,12},{30,14},{0,16},... | collective-permute-start | bytes 2359304 | tf_op jit(solution)/shard_map/ppermute | solution.py:32
where the time goes:
time: 191 us; the launch traced here: 190 us
  local copies, waits for them, and re-layouts  66.1 us (35%)
  waiting for transfers between devices  55.7 us (29%)
  matrix products  18.4 us (10%)
  loops' own time  18.3 us (10%)
  other arithmetic  11.7 us (6%)
  blocking collectives  9.63 us (5%)
  starting transfers between devices  9.62 us (5%)
    ppermute x2, waiting for transfers between devices, passed_along(): return lax.ppermute(block, axis, route)  33.7 us
    while x104, local copies, waits for them, and re-layouts  18.7 us
    another operation x2, loops' own time, correlate(): lax.scan(lag_block, 0, jnp.arange(LAGS // 5, dtype=jnp.int32))  18.3 us
    dynamic_update_slice x26, local copies, waits for them, and re-layouts, correlate(): lax.scan(lag_block, 0, jnp.arange(LAGS // 5, dtype=jnp.int32))  17.7 us
    dot_general x26, matrix products, lag_block(): lax.dot_general(stacked, partner, (((1,), (1,)), ((), ())), preferred_ele...  17.5 us
    dynamic_slice x26, local copies, waits for them, and re-layouts, correlate(): lax.scan(lag_block, 0, jnp.arange(LAGS // 5, dtype=jnp.int32))  16.3 us
    ppermute x2, waiting for transfers between devices, padded_2(): lax.ppermute(lax.slice_in_dim(block, block.shape[dim] - width, None, axis...  14.6 us
    all_gather x1, blocking collectives, on_device(): own_whole = lax.all_gather(normalized, 'ta', axis=1, tiled=True)  9.63 us
  transfers between devices with their start and end apart: 6, of which 4 were waited for; matrix products, arithmetic and copies ran while one was open for 23% of the time, Pallas kernels for 0%

commit v1 on v0

v1 whole, which is shorter than its diff:
```python
import functools
import math

import jax
import jax.numpy as jnp
from jax import lax
from jax.experimental import pallas as pl
from jax.experimental.pallas import tpu as pltpu
from jax.sharding import PartitionSpec as P

HF = 16
TAPS = 33
NBANDS = 4
LAGH = 32
LAGS = 65
ROUNDS = 2
FINE = 16
SUBS = 2
PADK = 128
MESH = pl.DeviceIdType.MESH
F32 = jnp.float32
BF16 = jnp.bfloat16


def split(x):
    high = x.astype(BF16)
    return high, (x - high.astype(F32)).astype(BF16)


def dot(a, b):
    return jnp.dot(a, b, preferred_element_type=F32)


def kernel(n_ta, n_ch, rows, length, raw_ref, band_ref, taps_ref, out_ref,
           x, xe, f, pre, suf, nbuf, own, shifted, qbuf, pt, acc, w_hi, w_lo, tri,
           local_sem, raw_send, raw_recv, z_send, q_recv, y_send, out_sem):
    a = lax.axis_index("ta")
    c = lax.axis_index("ch")
    off = n_ch // 4
    up = lax.rem(c + off, n_ch)
    down = lax.rem(c + n_ch - off, n_ch)
    whole = n_ta * length
    block = n_ta * rows
    chunk = length // SUBS
    n_chunks = n_ta * SUBS
    others = range(1, n_ta)

    def peer(p):
        return lax.rem(a + p, n_ta)

    def source(p):
        return lax.rem(a + n_ta - p, n_ta)

    def rows_of(g):
        return pl.ds(pl.multiple_of(g * rows, rows), rows)

    barrier = pltpu.get_barrier_semaphore()
    for target in (up, down):
        pl.semaphore_signal(barrier, inc=1, device_id=(target, a), device_id_type=MESH)
    for p in others:
        pl.semaphore_signal(barrier, inc=1, device_id=(c, peer(p)), device_id_type=MESH)
    pl.semaphore_wait(barrier, 2 + len(others))

    raw_copies = []
    for p in others:
        copy = pltpu.make_async_remote_copy(
            src_ref=raw_ref.at[rows_of(peer(p))], dst_ref=x.at[rows_of(a)],
            send_sem=raw_send.at[p], recv_sem=raw_recv.at[p],
            device_id=(c, peer(p)), device_id_type=MESH)
        copy.start()
        raw_copies.append(copy)
    mine = pltpu.make_async_copy(raw_ref.at[rows_of(a)], x.at[rows_of(a)], local_sem)
    mine.start()

    used = 160
    lane = lax.broadcasted_iota(jnp.int32, (used, 128), 1)
    row = lax.broadcasted_iota(jnp.int32, (used, 128), 0)
    diff = row - lane
    for b in range(NBANDS):
        w = jnp.zeros((used, 128), F32)
        for k in range(TAPS):
            w = jnp.where(diff == k, taps_ref[b, k], w)
        high, low = split(w)
        cols = slice(b * 128, (b + 1) * 128)
        w_hi[0:used, cols] = high
        w_lo[0:used, cols] = low
        w_hi[used:256, cols] = jnp.zeros((256 - used, 128), BF16)
        w_lo[used:256, cols] = jnp.zeros((256 - used, 128), BF16)
    r256 = lax.broadcasted_iota(jnp.int32, (256, 256), 0)
    c256 = lax.broadcasted_iota(jnp.int32, (256, 256), 1)
    tri[:, 0:256] = jnp.where(r256 <= c256, 1.0, 0.0).astype(BF16)
    tri[:, 256:512] = jnp.where(r256 >= c256, 1.0, 0.0).astype(BF16)
    pt[0:2 * LAGH, :] = jnp.zeros((2 * LAGH, ROUNDS * block), BF16)
    pt[2 * LAGH + whole:, :] = jnp.zeros((pt.shape[0] - 2 * LAGH - whole, ROUNDS * block), BF16)
    own[:, whole:] = jnp.zeros((rows, PADK), F32)

    bands = jnp.concatenate([band_ref[rows_of(a), :]] * n_ta, axis=0)
    bands = jnp.broadcast_to(bands, (block, 128))

    mine.wait()
    for p in others:
        pltpu.make_async_remote_copy(
            src_ref=x.at[rows_of(source(p))], dst_ref=x.at[rows_of(source(p))],
            send_sem=raw_send.at[p], recv_sem=raw_recv.at[p],
            device_id=(c, source(p)), device_id_type=MESH).wait_recv()

    xe[:, 128:128 + length] = x[...]
    zeros = jnp.zeros((rows, 128), F32)
    for g in range(n_ta):
        here = slice(g * rows, (g + 1) * rows)
        xe[here, 0:128] = x[(g - 1) * rows:g * rows, length - 128:] if g > 0 else zeros
        xe[here, 128 + length:] = x[(g + 1) * rows:(g + 2) * rows, 0:128] if g < n_ta - 1 else zeros
    moved = pltpu.roll(xe[...], 128 + length + 128 - (128 - HF), 1)
    x_hi, x_lo = split(moved)
    for n in range(length // 128):
        lanes = slice(128 * n, 128 * n + 256)
        res = dot(x_hi[:, lanes], w_hi[...]) + (dot(x_lo[:, lanes], w_hi[...]) + dot(x_hi[:, lanes], w_lo[...]))
        picked = res[:, 0:128]
        for b in range(1, NBANDS):
            picked = jnp.where(bands == b, res[:, b * 128:(b + 1) * 128], picked)
        f[:, 128 * n:128 * (n + 1)] = picked

    n_sum = length // 256
    total = jnp.zeros((block, 1), F32)
    totals = []
    for m in range(n_sum):
        lanes = slice(256 * m, 256 * (m + 1))
        high, low = split(jnp.abs(f[:, lanes]))
        res = dot(high, tri[...]) + dot(low, tri[...])
        pre[:, lanes] = res[:, 0:256] + total
        suf[:, lanes] = res[:, 256:512]
        part = res[:, 255:256]
        totals.append(part)
        total = total + part
    behind = jnp.zeros((block, 1), F32)
    for m in reversed(range(n_sum)):
        lanes = slice(256 * m, 256 * (m + 1))
        if m < n_sum - 1:
            behind = behind + totals[m + 1]
            suf[:, lanes] = suf[:, lanes] + behind

    z_copies = []
    for k in range(n_chunks):
        g, s = k // SUBS, k % SUBS
        lanes = slice(s * chunk, (s + 1) * chunk)
        here = slice(g * rows, (g + 1) * rows)
        window = jnp.broadcast_to(total[here], (rows, chunk))
        if g > 0:
            window = window + suf[(g - 1) * rows:g * rows, lanes]
        if g < n_ta - 1:
            window = window + pre[(g + 1) * rows:(g + 2) * rows, lanes]
        time = k * chunk + lax.broadcasted_iota(jnp.int32, (1, chunk), 1)
        counted = jnp.minimum(time + length, whole - 1) + 1 - jnp.maximum(time - length, 0)
        level = window * (1.0 / counted.astype(F32))
        normalized = (f[here, lanes] / (level + 1e-6)).astype(BF16)
        nbuf[k] = normalized
        own[:, k * chunk:(k + 1) * chunk] = normalized.astype(F32)
        copy = pltpu.make_async_remote_copy(
            src_ref=nbuf.at[k], dst_ref=qbuf.at[0, k, rows_of(a)],
            send_sem=z_send.at[0, k], recv_sem=q_recv.at[0, k, 0],
            device_id=(up, a), device_id_type=MESH)
        copy.start()
        z_copies.append(copy)

    step = min(rows, 16)
    for i in range(rows // step):
        part = own[i * step:(i + 1) * step, :]
        for fine in range(FINE):
            shifted[fine * rows + i * step:fine * rows + (i + 1) * step, :] = (
                pltpu.roll(part, LAGH + fine, 1).astype(BF16))

    y_copies = []

    def arrived(r, k, p):
        slot = qbuf.at[r, k, rows_of(source(p))]
        pltpu.make_async_remote_copy(
            src_ref=slot, dst_ref=slot, send_sem=z_send.at[0, k], recv_sem=q_recv.at[r, k, p],
            device_id=(c, a), device_id_type=MESH).wait_recv()

    def forward(r, k):
        arrived(r, k, 0)
        slot = (r, k, rows_of(a))
        if r + 1 < ROUNDS:
            copy = pltpu.make_async_remote_copy(
                src_ref=qbuf.at[slot], dst_ref=qbuf.at[r + 1, k, rows_of(a)],
                send_sem=z_send.at[r + 1, k], recv_sem=q_recv.at[r + 1, k, 0],
                device_id=(up, a), device_id_type=MESH)
            copy.start()
            z_copies.append(copy)
        for p in others:
            copy = pltpu.make_async_remote_copy(
                src_ref=qbuf.at[slot], dst_ref=qbuf.at[slot],
                send_sem=y_send.at[r, k, p], recv_sem=q_recv.at[r, k, p],
                device_id=(c, peer(p)), device_id_type=MESH)
            copy.start()
            y_copies.append(copy)

    scale = 1.0 / math.sqrt(whole)
    half = FINE // 2
    coarse = LAGS // FINE

    def correlate(k):
        for r in range(ROUNDS):
            for p in others:
                arrived(r, k, p)
            pt[2 * LAGH + k * chunk:2 * LAGH + (k + 1) * chunk, r * block:(r + 1) * block] = qbuf[r, k].T
        first, last = k == 0, k == n_chunks - 1
        begin = k * chunk
        depth = chunk + (PADK if last else 0)

        def piece(lag0, n_lags, row0, shift):
            res = dot(shifted[pl.ds(row0, n_lags * rows), begin:begin + depth],
                      pt[pl.ds(begin + shift, depth), :])
            for r in range(ROUNDS):
                part = res[:, r * block:(r + 1) * block].reshape(n_lags, rows, block)
                where = (r, pl.ds(lag0, n_lags))
                if not first:
                    part = acc[where] + part
                acc[where] = part * scale if last else part

        def send(lag0, n_lags, slot):
            return pltpu.make_async_copy(
                acc.at[:, pl.ds(lag0, n_lags)], out_ref.at[:, pl.ds(lag0, n_lags)], out_sem.at[slot])

        def body(i, carry):
            b, h = i // 2, i % 2
            piece(i * half, half, pl.multiple_of(h * (half * rows), half * rows),
                  pl.multiple_of(b * FINE, FINE))
            if last:
                send(i * half, half, i).start()
            return carry

        lax.fori_loop(0, 2 * coarse, body, 0)
        piece(coarse * FINE, 1, 0, coarse * FINE)
        if last:
            send(coarse * FINE, 1, 2 * coarse).start()
            for i in range(2 * coarse):
                send(i * half, half, i).wait()
            send(coarse * FINE, 1, 2 * coarse).wait()

    for turn in range(n_chunks + 2):
        if turn < n_chunks:
            forward(0, turn)
        if 0 <= turn - 1 < n_chunks:
            forward(1, turn - 1)
        if turn - 2 >= 0:
            correlate(turn - 2)

    for copy in raw_copies + z_copies + y_copies:
        copy.wait_send()


def on_device(n_ta, n_ch, raw_strain, band_index, filter_taps):
    block, length = raw_strain.shape
    rows = block // n_ta
    whole = n_ta * length
    chunk = length // SUBS
    n_chunks = n_ta * SUBS
    dma = pltpu.SemaphoreType.DMA
    return pl.pallas_call(
        functools.partial(kernel, n_ta, n_ch, rows, length),
        out_shape=jax.ShapeDtypeStruct((ROUNDS, LAGS, rows, block), F32),
        in_specs=[
            pl.BlockSpec(memory_space=pl.ANY),
            pl.BlockSpec(memory_space=pltpu.VMEM),
            pl.BlockSpec(memory_space=pltpu.SMEM),
        ],
        out_specs=pl.BlockSpec(memory_space=pl.ANY),
        scratch_shapes=[
            pltpu.VMEM((block, length), F32),
            pltpu.VMEM((block, length + 256), F32),
            pltpu.VMEM((block, length), F32),
            pltpu.VMEM((block, length), F32),
            pltpu.VMEM((block, length), F32),
            pltpu.VMEM((n_chunks, rows, chunk), BF16),
            pltpu.VMEM((rows, whole + PADK), F32),
            pltpu.VMEM((FINE * rows, whole + PADK), BF16),
            pltpu.VMEM((ROUNDS, n_chunks, block, chunk), BF16),
            pltpu.VMEM((2 * LAGH + whole + PADK, ROUNDS * block), BF16),
            pltpu.VMEM((ROUNDS, LAGS, rows, block), F32),
            pltpu.VMEM((256, NBANDS * 128), BF16),
            pltpu.VMEM((256, NBANDS * 128), BF16),
            pltpu.VMEM((256, 512), BF16),
            dma(()),
            dma((n_ta,)),
            dma((n_ta,)),
            dma((ROUNDS, n_chunks)),
            dma((ROUNDS, n_chunks, n_ta)),
            dma((ROUNDS, n_chunks, n_ta)),
            dma((2 * (LAGS // FINE) + 1,)),
        ],
        compiler_params=pltpu.CompilerParams(
            collective_id=0, has_side_effects=True, vmem_limit_bytes=56 * 1024 * 1024),
    )(raw_strain, band_index.reshape(block, 1), filter_taps)


def solution(mesh):
    placed = (P("ch", "ta"), P("ch"), P())
    return jax.shard_map(
        functools.partial(on_device, mesh.shape["ta"], mesh.shape["ch"]),
        mesh=mesh,
        in_specs=placed,
        out_specs=P(None, None, ("ch", "ta"), None),
        check_vma=False,
    )
```

time: 191 us -> 57.6 us (0.30)
  the two profiles are of different devices: /device:TPU:18 before, /device:TPU:0 now
where the time goes in v1:
time: 57.6 us; the launch traced here: 57.3 us
  Pallas kernels  51.1 us (89%)
  local copies, waits for them, and re-layouts  6.23 us (11%)
    pallas_call x1, Pallas kernels, on_device(): pl.pallas_call(functools.partial(kernel, n_ta, n_ch, rows, length), out_s...  51.1 us
    unnamed x1, local copies, waits for them, and re-layouts  4.84 us
    reshape x1, local copies, waits for them, and re-layouts, on_device(): band_index.reshape(block, 1)  1.39 us

profile of v1, /device:TPU:0, one launch (start us, length us, event | category | flops | bytes accessed | tf_op | source)
XLA Modules:
  0.0 57.3 jit_solution(2703893558693032731)
XLA Ops:
  0.0 1.4 %copy.4.band_ref = s32[128,1]{1,0:T(8,128)} copy(s32[128,1]{0,1:T(1,128)} %bitcast.1) | data formatting | bytes 1024 | tf_op jit(solution)/shard_map/reshape | solution.py:294
  1.4 51.1 %shard_map.37 = f32[2,65,64,128]{3,2,1,0:T(8,128)} custom-call(f32[128,1536]{1,0:T(8,128)} %raw_ref.1, s32[128,1]{1,0:T(8,128)} %copy.4.band_ref, f32[4,33]{1,0:T(4,128)} %taps_ref.1), custom_call_target="tpu_custom_call" | custom-call | tf_op jit(solution)/shard_map/pallas_call | solution.py:260
  52.5 4.8 %copy.6 = f32[2,65,64,128]{3,2,1,0:T(8,128)} copy(f32[2,65,64,128]{3,2,1,0:T(8,128)} %shard_map.37) | data formatting | bytes 8519680

commit v2 on v1

--- a/solution.py
+++ b/solution.py
@@ -32,7 +32,7 @@
 
 
 def kernel(n_ta, n_ch, rows, length, raw_ref, band_ref, taps_ref, out_ref,
-           x, xe, f, pre, suf, nbuf, own, shifted, qbuf, pt, acc, w_hi, w_lo, tri,
+           x, xe, f, pre, suf, nbuf, own, shifted, qbuf, pt, acc, w_hi, w_lo, tri, xs_hi, xs_lo,
            local_sem, raw_send, raw_recv, z_send, q_recv, y_send, out_sem):
     a = lax.axis_index("ta")
     c = lax.axis_index("ch")
@@ -92,9 +92,11 @@
     tri[:, 256:512] = jnp.where(r256 >= c256, 1.0, 0.0).astype(BF16)
     pt[0:2 * LAGH, :] = jnp.zeros((2 * LAGH, ROUNDS * block), BF16)
     pt[2 * LAGH + whole:, :] = jnp.zeros((pt.shape[0] - 2 * LAGH - whole, ROUNDS * block), BF16)
-    own[:, whole:] = jnp.zeros((rows, PADK), F32)
-
-    bands = jnp.concatenate([band_ref[rows_of(a), :]] * n_ta, axis=0)
+    own[:, whole:] = jnp.zeros((rows, PADK), BF16)
+
+    row = lax.broadcasted_iota(jnp.int32, (block, block), 0)
+    chosen = lax.broadcasted_iota(jnp.int32, (block, block), 1) == a * rows + lax.rem(row, rows)
+    bands = jnp.sum(jnp.where(chosen, band_ref[...].astype(F32), 0.0), axis=1, keepdims=True)
     bands = jnp.broadcast_to(bands, (block, 128))
 
     mine.wait()
@@ -114,11 +116,17 @@
     x_hi, x_lo = split(moved)
     for n in range(length // 128):
         lanes = slice(128 * n, 128 * n + 256)
-        res = dot(x_hi[:, lanes], w_hi[...]) + (dot(x_lo[:, lanes], w_hi[...]) + dot(x_hi[:, lanes], w_lo[...]))
-        picked = res[:, 0:128]
-        for b in range(1, NBANDS):
-            picked = jnp.where(bands == b, res[:, b * 128:(b + 1) * 128], picked)
-        f[:, 128 * n:128 * (n + 1)] = picked
+        xs_hi[n * block:(n + 1) * block, :] = x_hi[:, lanes]
+        xs_lo[n * block:(n + 1) * block, :] = x_lo[:, lanes]
+    for m in range(length // 512):
+        part = slice(4 * m * block, 4 * (m + 1) * block)
+        res = dot(xs_hi[part, :], w_hi[...]) + (dot(xs_lo[part, :], w_hi[...]) + dot(xs_hi[part, :], w_lo[...]))
+        for q in range(4):
+            one = res[q * block:(q + 1) * block]
+            picked = one[:, 0:128]
+            for b in range(1, NBANDS):
+                picked = jnp.where(bands == float(b), one[:, b * 128:(b + 1) * 128], picked)
+            f[:, 128 * (4 * m + q):128 * (4 * m + q + 1)] = picked
 
     n_sum = length // 256
     total = jnp.zeros((block, 1), F32)
@@ -154,7 +162,7 @@
         level = window * (1.0 / counted.astype(F32))
         normalized = (f[here, lanes] / (level + 1e-6)).astype(BF16)
         nbuf[k] = normalized
-        own[:, k * chunk:(k + 1) * chunk] = normalized.astype(F32)
+        own[:, k * chunk:(k + 1) * chunk] = normalized
         copy = pltpu.make_async_remote_copy(
             src_ref=nbuf.at[k], dst_ref=qbuf.at[0, k, rows_of(a)],
             send_sem=z_send.at[0, k], recv_sem=q_recv.at[0, k, 0],
@@ -163,7 +171,9 @@
         z_copies.append(copy)
 
     step = min(rows, 16)
-    for i in range(rows // step):
+    n_parts = rows // step
+
+    def shift_part(i):
         part = own[i * step:(i + 1) * step, :]
         for fine in range(FINE):
             shifted[fine * rows + i * step:fine * rows + (i + 1) * step, :] = (
@@ -238,13 +248,17 @@
                 send(i * half, half, i).wait()
             send(coarse * FINE, 1, 2 * coarse).wait()
 
-    for turn in range(n_chunks + 2):
+    delay = max(2, n_parts - 1)
+    shift_part(0)
+    for turn in range(n_chunks + delay):
         if turn < n_chunks:
             forward(0, turn)
         if 0 <= turn - 1 < n_chunks:
             forward(1, turn - 1)
-        if turn - 2 >= 0:
-            correlate(turn - 2)
+        if turn + 1 < n_parts:
+            shift_part(turn + 1)
+        if turn - delay >= 0:
+            correlate(turn - delay)
 
     for copy in raw_copies + z_copies + y_copies:
         copy.wait_send()
@@ -273,7 +287,7 @@
             pltpu.VMEM((block, length), F32),
             pltpu.VMEM((block, length), F32),
             pltpu.VMEM((n_chunks, rows, chunk), BF16),
-            pltpu.VMEM((rows, whole + PADK), F32),
+            pltpu.VMEM((rows, whole + PADK), BF16),
             pltpu.VMEM((FINE * rows, whole + PADK), BF16),
             pltpu.VMEM((ROUNDS, n_chunks, block, chunk), BF16),
             pltpu.VMEM((2 * LAGH + whole + PADK, ROUNDS * block), BF16),
@@ -281,6 +295,8 @@
             pltpu.VMEM((256, NBANDS * 128), BF16),
             pltpu.VMEM((256, NBANDS * 128), BF16),
             pltpu.VMEM((256, 512), BF16),
+            pltpu.VMEM((length // 128 * block, 256), BF16),
+            pltpu.VMEM((length // 128 * block, 256), BF16),
             dma(()),
             dma((n_ta,)),
             dma((n_ta,)),
@@ -290,8 +306,8 @@
             dma((2 * (LAGS // FINE) + 1,)),
         ],
         compiler_params=pltpu.CompilerParams(
-            collective_id=0, has_side_effects=True, vmem_limit_bytes=56 * 1024 * 1024),
-    )(raw_strain, band_index.reshape(block, 1), filter_taps)
+            collective_id=0, has_side_effects=True, vmem_limit_bytes=32 * 1024 * 1024),
+    )(raw_strain, band_index.reshape(1, block), filter_taps)
 
 
 def solution(mesh):

time: 57.6 us -> 55.6 us (0.965)
  local copies, waits for them, and re-layouts: 6.23 us -> 4.51 us
    reshape x1 -> x0, local copies, waits for them, and re-layouts: 1.39 us -> none  [on_device(): band_index.reshape(block, 1)]
    unnamed x1 -> x7, local copies, waits for them, and re-layouts: 4.84 us -> 4.51 us
where the time goes in v2:
time: 55.6 us; the launch traced here: 55.5 us
  Pallas kernels  50.9 us (92%)
  local copies, waits for them, and re-layouts  4.51 us (8%)
    pallas_call x1, Pallas kernels, on_device(): pl.pallas_call(functools.partial(kernel, n_ta, n_ch, rows, length), out_s...  50.9 us
    unnamed x7, local copies, waits for them, and re-layouts  4.51 us

profile of v2, /device:TPU:0, one launch (start us, length us, event | category | flops | bytes accessed | tf_op | source)
XLA Modules:
  0.0 55.5 jit_solution(12295424113188791749)
XLA Ops:
  0.0 0.0 copy-start
  0.0 1.1 %copy-done = f32[128,1536]{1,0:T(8,128)S(1)} copy-done((f32[128,1536]{1,0:T(8,128)S(1)}, f32[128,1536]{1,0:T(8,128)}, u32[]{:S(2)}) %copy-start) | copy-done | bytes 786456
  1.1 0.0 copy-start.1
  1.1 0.7 %copy-done.1 = f32[4,33]{1,0:T(4,128)S(1)} copy-done((f32[4,33]{1,0:T(4,128)S(1)}, f32[4,33]{1,0:T(4,128)}, u32[]{:S(2)}) %copy-start.1) | copy-done | bytes 552
  1.8 0.0 copy-start.2
  1.8 0.7 %copy-done.2 = s32[128]{0:T(128)S(1)} copy-done((s32[128]{0:T(128)S(1)}, s32[128]{0:T(128)}, u32[]{:S(2)}) %copy-start.2) | copy-done | bytes 536
  2.5 50.9 %shard_map.37 = f32[2,65,64,128]{3,2,1,0:T(8,128)S(1)} custom-call(f32[128,1536]{1,0:T(8,128)S(1)} %copy-done, s32[1,128]{1,0:T(1,128)S(1)} %bitcast.1, f32[4,33]{1,0:T(4,128)S(1)} %copy-done.1), custom_call_target="tpu_custom_call" | custom-call | tf_op jit(solution)/shard_map/pallas_call | solution.py:274
  53.4 2.0 %copy.5 = f32[2,65,64,128]{3,2,1,0:T(8,128)} copy(f32[2,65,64,128]{3,2,1,0:T(8,128)S(1)} %shard_map.37) | data formatting | bytes 8519680
Async XLA Ops:
  0.0 1.1 %copy-start = (f32[128,1536]{1,0:T(8,128)S(1)}, f32[128,1536]{1,0:T(8,128)}, u32[]{:S(2)}) copy-start(f32[128,1536]{1,0:T(8,128)} %raw_ref.1) | copy-start | bytes 2359300
  1.1 0.7 %copy-start.1 = (f32[4,33]{1,0:T(4,128)S(1)}, f32[4,33]{1,0:T(4,128)}, u32[]{:S(2)}) copy-start(f32[4,33]{1,0:T(4,128)} %taps_ref.1) | copy-start | bytes 1588
  1.8 0.7 %copy-start.2 = (s32[128]{0:T(128)S(1)}, s32[128]{0:T(128)}, u32[]{:S(2)}) copy-start(s32[128]{0:T(128)} %param.4) | copy-start | bytes 1540

commit v3 on v1

v3 whole, which is shorter than its diff:
```python
import functools
import math

import jax
import jax.numpy as jnp
from jax import lax
from jax.experimental import pallas as pl
from jax.experimental.pallas import tpu as pltpu
from jax.sharding import PartitionSpec as P

HF = 16
TAPS = 33
NBANDS = 4
LAGH = 32
LAGS = 65
ROUNDS = 2
FINE = 16
SUBS = 2
PARTS = 2
PADK = 128
MESH = pl.DeviceIdType.MESH
F32 = jnp.float32
BF16 = jnp.bfloat16


def split(x):
    high = x.astype(BF16)
    return high, (x - high.astype(F32)).astype(BF16)


def dot(a, b):
    return jnp.dot(a, b, preferred_element_type=F32)


def kernel(n_ta, n_ch, rows, length, n_parts, raw_ref, band_hbm, taps_hbm, out_ref,
           band_ref, taps_ref, x, xe, f, pre, suf, nbuf, own, shifted, qbuf, pt, acc, w_hi, w_lo, tri, xs_hi, xs_lo,
           small_sem, local_sem, raw_send, raw_recv, z_send, q_recv, y_send, out_sem):
    a = lax.axis_index("ta")
    c = lax.axis_index("ch")
    off = n_ch // 4
    up = lax.rem(c + off, n_ch)
    down = lax.rem(c + n_ch - off, n_ch)
    whole = n_ta * length
    block = n_ta * rows
    hr = rows // n_parts
    tall = n_ta * hr
    chunk = length // SUBS
    n_chunks = n_ta * SUBS
    others = range(1, n_ta)

    def peer(p):
        return lax.rem(a + p, n_ta)

    def source(p):
        return lax.rem(a + n_ta - p, n_ta)

    def rows_of(g, h):
        return pl.ds(pl.multiple_of(g * rows + h * hr, hr), hr)

    def place(g):
        return pl.ds(pl.multiple_of(g * hr, hr), hr)

    small = [pltpu.make_async_copy(band_hbm, band_ref, small_sem.at[0]),
             pltpu.make_async_copy(taps_hbm, taps_ref, small_sem.at[1])]
    mine = [pltpu.make_async_copy(raw_ref.at[rows_of(a, h)], x.at[h, place(a)], local_sem.at[h])
            for h in range(n_parts)]
    for copy in small + mine:
        copy.start()

    barrier = pltpu.get_barrier_semaphore()
    for target in (up, down):
        pl.semaphore_signal(barrier, inc=1, device_id=(target, a), device_id_type=MESH)
    for p in others:
        pl.semaphore_signal(barrier, inc=1, device_id=(c, peer(p)), device_id_type=MESH)
    pl.semaphore_wait(barrier, 2 + len(others))

    raw_copies = []
    for h in range(n_parts):
        for p in others:
            copy = pltpu.make_async_remote_copy(
                src_ref=raw_ref.at[rows_of(peer(p), h)], dst_ref=x.at[h, place(a)],
                send_sem=raw_send.at[h, p], recv_sem=raw_recv.at[h, p],
                device_id=(c, peer(p)), device_id_type=MESH)
            copy.start()
            raw_copies.append(copy)
    for copy in small:
        copy.wait()

    used = 160
    lane = lax.broadcasted_iota(jnp.int32, (used, 128), 1)
    row = lax.broadcasted_iota(jnp.int32, (used, 128), 0)
    diff = row - lane
    for b in range(NBANDS):
        w = jnp.zeros((used, 128), F32)
        for k in range(TAPS):
            w = jnp.where(diff == k, taps_ref[b, k], w)
        high, low = split(w)
        cols = slice(b * 128, (b + 1) * 128)
        w_hi[0:used, cols] = high
        w_lo[0:used, cols] = low
        w_hi[used:256, cols] = jnp.zeros((256 - used, 128), BF16)
        w_lo[used:256, cols] = jnp.zeros((256 - used, 128), BF16)
    r256 = lax.broadcasted_iota(jnp.int32, (256, 256), 0)
    c256 = lax.broadcasted_iota(jnp.int32, (256, 256), 1)
    tri[:, 0:256] = jnp.where(r256 <= c256, 1.0, 0.0).astype(BF16)
    tri[:, 256:512] = jnp.where(r256 >= c256, 1.0, 0.0).astype(BF16)
    pt[0:2 * LAGH, :] = jnp.zeros((2 * LAGH, ROUNDS * block), BF16)
    pt[2 * LAGH + whole:, :] = jnp.zeros((pt.shape[0] - 2 * LAGH - whole, ROUNDS * block), BF16)
    own[:, whole:] = jnp.zeros((rows, PADK), BF16)

    z_copies = []

    def prepare(h):
        row = lax.broadcasted_iota(jnp.int32, (tall, block), 0)
        chosen = lax.broadcasted_iota(jnp.int32, (tall, block), 1) == a * rows + h * hr + lax.rem(row, hr)
        bands = jnp.sum(jnp.where(chosen, band_ref[...].astype(F32), 0.0), axis=1, keepdims=True)
        bands = jnp.broadcast_to(bands, (tall, 128))

        mine[h].wait()
        for p in others:
            slot = x.at[h, place(source(p))]
            pltpu.make_async_remote_copy(
                src_ref=slot, dst_ref=slot,
                send_sem=raw_send.at[h, p], recv_sem=raw_recv.at[h, p],
                device_id=(c, source(p)), device_id_type=MESH).wait_recv()

        xe[:, 128:128 + length] = x[h]
        zeros = jnp.zeros((hr, 128), F32)
        for g in range(n_ta):
            here = slice(g * hr, (g + 1) * hr)
            xe[here, 0:128] = x[h, (g - 1) * hr:g * hr, length - 128:] if g > 0 else zeros
            xe[here, 128 + length:] = x[h, (g + 1) * hr:(g + 2) * hr, 0:128] if g < n_ta - 1 else zeros
        moved = pltpu.roll(xe[...], 128 + length + 128 - (128 - HF), 1)
        x_hi, x_lo = split(moved)
        for n in range(length // 128):
            lanes = slice(128 * n, 128 * n + 256)
            xs_hi[n * tall:(n + 1) * tall, :] = x_hi[:, lanes]
            xs_lo[n * tall:(n + 1) * tall, :] = x_lo[:, lanes]
        for m in range(length // 512):
            part = slice(4 * m * tall, 4 * (m + 1) * tall)
            res = dot(xs_hi[part, :], w_hi[...]) + (dot(xs_lo[part, :], w_hi[...]) + dot(xs_hi[part, :], w_lo[...]))
            for q in range(4):
                one = res[q * tall:(q + 1) * tall]
                picked = one[:, 0:128]
                for b in range(1, NBANDS):
                    picked = jnp.where(bands == float(b), one[:, b * 128:(b + 1) * 128], picked)
                f[:, 128 * (4 * m + q):128 * (4 * m + q + 1)] = picked

        n_sum = length // 256
        total = jnp.zeros((tall, 1), F32)
        totals = []
        for m in range(n_sum):
            lanes = slice(256 * m, 256 * (m + 1))
            high, low = split(jnp.abs(f[:, lanes]))
            res = dot(high, tri[...]) + dot(low, tri[...])
            pre[:, lanes] = res[:, 0:256] + total
            suf[:, lanes] = res[:, 256:512]
            part = res[:, 255:256]
            totals.append(part)
            total = total + part
        behind = jnp.zeros((tall, 1), F32)
        for m in reversed(range(n_sum)):
            lanes = slice(256 * m, 256 * (m + 1))
            if m < n_sum - 1:
                behind = behind + totals[m + 1]
                suf[:, lanes] = suf[:, lanes] + behind

        ours = slice(h * hr, (h + 1) * hr)
        for k in range(n_chunks):
            g, s = k // SUBS, k % SUBS
            lanes = slice(s * chunk, (s + 1) * chunk)
            here = slice(g * hr, (g + 1) * hr)
            window = jnp.broadcast_to(total[here], (hr, chunk))
            if g > 0:
                window = window + suf[(g - 1) * hr:g * hr, lanes]
            if g < n_ta - 1:
                window = window + pre[(g + 1) * hr:(g + 2) * hr, lanes]
            time = k * chunk + lax.broadcasted_iota(jnp.int32, (1, chunk), 1)
            counted = jnp.minimum(time + length, whole - 1) + 1 - jnp.maximum(time - length, 0)
            level = window * (1.0 / counted.astype(F32))
            normalized = (f[here, lanes] / (level + 1e-6)).astype(BF16)
            nbuf[k, ours] = normalized
            own[ours, k * chunk:(k + 1) * chunk] = normalized
            copy = pltpu.make_async_remote_copy(
                src_ref=nbuf.at[k, ours], dst_ref=qbuf.at[0, k, rows_of(a, h)],
                send_sem=z_send.at[0, k, h], recv_sem=q_recv.at[0, k, h, 0],
                device_id=(up, a), device_id_type=MESH)
            copy.start()
            z_copies.append(copy)

    step = min(rows, 16)
    n_shift = rows // step

    def shift_part(i):
        part = own[i * step:(i + 1) * step, :]
        for fine in range(FINE):
            shifted[fine * rows + i * step:fine * rows + (i + 1) * step, :] = (
                pltpu.roll(part, LAGH + fine, 1).astype(BF16))

    y_copies = []

    def arrived(r, k, h, p):
        slot = qbuf.at[r, k, rows_of(source(p), h)]
        pltpu.make_async_remote_copy(
            src_ref=slot, dst_ref=slot, send_sem=z_send.at[0, k, h], recv_sem=q_recv.at[r, k, h, p],
            device_id=(c, a), device_id_type=MESH).wait_recv()

    def forward(r, k, h):
        arrived(r, k, h, 0)
        slot = (r, k, rows_of(a, h))
        if r + 1 < ROUNDS:
            copy = pltpu.make_async_remote_copy(
                src_ref=qbuf.at[slot], dst_ref=qbuf.at[r + 1, k, rows_of(a, h)],
                send_sem=z_send.at[r + 1, k, h], recv_sem=q_recv.at[r + 1, k, h, 0],
                device_id=(up, a), device_id_type=MESH)
            copy.start()
            z_copies.append(copy)
        for p in others:
            copy = pltpu.make_async_remote_copy(
                src_ref=qbuf.at[slot], dst_ref=qbuf.at[slot],
                send_sem=y_send.at[r, k, h, p], recv_sem=q_recv.at[r, k, h, p],
                device_id=(c, peer(p)), device_id_type=MESH)
            copy.start()
            y_copies.append(copy)

    scale = 1.0 / math.sqrt(whole)
    half = FINE // 2
    coarse = LAGS // FINE

    def correlate(k):
        for r in range(ROUNDS):
            for h in range(n_parts):
                for p in others:
                    arrived(r, k, h, p)
            pt[2 * LAGH + k * chunk:2 * LAGH + (k + 1) * chunk, r * block:(r + 1) * block] = qbuf[r, k].T
        first, last = k == 0, k == n_chunks - 1
        begin = k * chunk
        depth = chunk + (PADK if last else 0)

        def piece(lag0, n_lags, row0, shift):
            res = dot(shifted[pl.ds(row0, n_lags * rows), begin:begin + depth],
                      pt[pl.ds(begin + shift, depth), :])
            for r in range(ROUNDS):
                part = res[:, r * block:(r + 1) * block].reshape(n_lags, rows, block)
                where = (r, pl.ds(lag0, n_lags))
                if not first:
                    part = acc[where] + part
                acc[where] = part * scale if last else part

        def send(lag0, n_lags, slot):
            return pltpu.make_async_copy(
                acc.at[:, pl.ds(lag0, n_lags)], out_ref.at[:, pl.ds(lag0, n_lags)], out_sem.at[slot])

        def body(i, carry):
            b, h = i // 2, i % 2
            piece(i * half, half, pl.multiple_of(h * (half * rows), half * rows),
                  pl.multiple_of(b * FINE, FINE))
            if last:
                send(i * half, half, i).start()
            return carry

        lax.fori_loop(0, 2 * coarse, body, 0)
        piece(coarse * FINE, 1, 0, coarse * FINE)
        if last:
            send(coarse * FINE, 1, 2 * coarse).start()
            for i in range(2 * coarse):
                send(i * half, half, i).wait()
            send(coarse * FINE, 1, 2 * coarse).wait()

    for h in range(n_parts):
        prepare(h)
    tail = n_parts - 1
    for h in range(tail):
        for k in range(n_chunks):
            forward(0, k, h)
    early = n_shift // 2
    for i in range(early):
        shift_part(i)
    delay = max(2, n_shift - early - 1)
    for turn in range(n_chunks + delay):
        if turn < n_chunks:
            forward(0, turn, tail)
            for h in range(tail):
                forward(1, turn, h)
        if 0 <= turn - 1 < n_chunks:
            forward(1, turn - 1, tail)
        if early + turn < n_shift:
            shift_part(early + turn)
        if turn - delay >= 0:
            correlate(turn - delay)

    for copy in raw_copies + z_copies + y_copies:
        copy.wait_send()


def on_device(n_ta, n_ch, raw_strain, band_index, filter_taps):
    block, length = raw_strain.shape
    rows = block // n_ta
    whole = n_ta * length
    chunk = length // SUBS
    n_chunks = n_ta * SUBS
    n_parts = max(1, min(PARTS, rows // 16))
    tall = block // n_parts
    dma = pltpu.SemaphoreType.DMA
    return pl.pallas_call(
        functools.partial(kernel, n_ta, n_ch, rows, length, n_parts),
        out_shape=jax.ShapeDtypeStruct((ROUNDS, LAGS, rows, block), F32),
        in_specs=[
            pl.BlockSpec(memory_space=pltpu.HBM),
            pl.BlockSpec(memory_space=pltpu.HBM),
            pl.BlockSpec(memory_space=pltpu.HBM),
        ],
        out_specs=pl.BlockSpec(memory_space=pl.ANY),
        scratch_shapes=[
            pltpu.VMEM((1, block), jnp.int32),
            pltpu.SMEM((NBANDS, TAPS), F32),
            pltpu.VMEM((n_parts, tall, length), F32),
            pltpu.VMEM((tall, length + 256), F32),
            pltpu.VMEM((tall, length), F32),
            pltpu.VMEM((tall, length), F32),
            pltpu.VMEM((tall, length), F32),
            pltpu.VMEM((n_chunks, rows, chunk), BF16),
            pltpu.VMEM((rows, whole + PADK), BF16),
            pltpu.VMEM((FINE * rows, whole + PADK), BF16),
            pltpu.VMEM((ROUNDS, n_chunks, block, chunk), BF16),
            pltpu.VMEM((2 * LAGH + whole + PADK, ROUNDS * block), BF16),
            pltpu.VMEM((ROUNDS, LAGS, rows, block), F32),
            pltpu.VMEM((256, NBANDS * 128), BF16),
            pltpu.VMEM((256, NBANDS * 128), BF16),
            pltpu.VMEM((256, 512), BF16),
            pltpu.VMEM((length // 128 * tall, 256), BF16),
            pltpu.VMEM((length // 128 * tall, 256), BF16),
            dma((2,)),
            dma((n_parts,)),
            dma((n_parts, n_ta)),
            dma((n_parts, n_ta)),
            dma((ROUNDS, n_chunks, n_parts)),
            dma((ROUNDS, n_chunks, n_parts, n_ta)),
            dma((ROUNDS, n_chunks, n_parts, n_ta)),
            dma((2 * (LAGS // FINE) + 1,)),
        ],
        compiler_params=pltpu.CompilerParams(
            collective_id=0, has_side_effects=True, vmem_limit_bytes=32 * 1024 * 1024),
    )(raw_strain, band_index.reshape(1, block), filter_taps)


def solution(mesh):
    placed = (P("ch", "ta"), P("ch"), P())
    return jax.shard_map(
        functools.partial(on_device, mesh.shape["ta"], mesh.shape["ch"]),
        mesh=mesh,
        in_specs=placed,
        out_specs=P(None, None, ("ch", "ta"), None),
        check_vma=False,
    )
```

time: 57.6 us -> 52.9 us (0.918)
  Pallas kernels: 51.1 us -> 48.2 us
  local copies, waits for them, and re-layouts: 6.23 us -> 4.51 us
    pallas_call x1, Pallas kernels: 51.1 us -> 48.2 us  [on_device(): pl.pallas_call(functools.partial(kernel, n_ta, n_ch, rows, length, n_part...]
    reshape x1 -> x0, local copies, waits for them, and re-layouts: 1.39 us -> none  [on_device(): band_index.reshape(block, 1)]
    unnamed x1 -> x7, local copies, waits for them, and re-layouts: 4.84 us -> 4.51 us
where the time goes in v3:
time: 52.9 us; the launch traced here: 52.7 us
  Pallas kernels  48.2 us (91%)
  local copies, waits for them, and re-layouts  4.51 us (9%)
    pallas_call x1, Pallas kernels, on_device(): pl.pallas_call(functools.partial(kernel, n_ta, n_ch, rows, length, n_part...  48.2 us
    unnamed x7, local copies, waits for them, and re-layouts  4.51 us

profile of v3, /device:TPU:0, one launch (start us, length us, event | category | flops | bytes accessed | tf_op | source)
XLA Modules:
  0.0 52.7 jit_solution(17553922552367787478)
XLA Ops:
  0.0 0.0 copy-start
  0.0 1.1 %copy-done = f32[128,1536]{1,0:T(8,128)S(1)} copy-done((f32[128,1536]{1,0:T(8,128)S(1)}, f32[128,1536]{1,0:T(8,128)}, u32[]{:S(2)}) %copy-start) | copy-done | bytes 786456
  1.1 0.0 copy-start.1
  1.1 0.7 %copy-done.1 = f32[4,33]{1,0:T(4,128)S(1)} copy-done((f32[4,33]{1,0:T(4,128)S(1)}, f32[4,33]{1,0:T(4,128)}, u32[]{:S(2)}) %copy-start.1) | copy-done | bytes 552
  1.8 0.0 copy-start.2
  1.8 0.7 %copy-done.2 = s32[128]{0:T(128)S(1)} copy-done((s32[128]{0:T(128)S(1)}, s32[128]{0:T(128)}, u32[]{:S(2)}) %copy-start.2) | copy-done | bytes 536
  2.5 48.2 %shard_map.37 = f32[2,65,64,128]{3,2,1,0:T(8,128)S(1)} custom-call(f32[128,1536]{1,0:T(8,128)S(1)} %copy-done, s32[1,128]{1,0:T(1,128)S(1)} %bitcast.1, f32[4,33]{1,0:T(4,128)S(1)} %copy-done.1), custom_call_target="tpu_custom_call" | custom-call | tf_op jit(solution)/shard_map/pallas_call | solution.py:305
  50.6 2.0 %copy.5 = f32[2,65,64,128]{3,2,1,0:T(8,128)} copy(f32[2,65,64,128]{3,2,1,0:T(8,128)S(1)} %shard_map.37) | data formatting | bytes 8519680
Async XLA Ops:
  0.0 1.1 %copy-start = (f32[128,1536]{1,0:T(8,128)S(1)}, f32[128,1536]{1,0:T(8,128)}, u32[]{:S(2)}) copy-start(f32[128,1536]{1,0:T(8,128)} %raw_ref.1) | copy-start | bytes 2359300
  1.1 0.7 %copy-start.1 = (f32[4,33]{1,0:T(4,128)S(1)}, f32[4,33]{1,0:T(4,128)}, u32[]{:S(2)}) copy-start(f32[4,33]{1,0:T(4,128)} %taps_hbm.1) | copy-start | bytes 1588
  1.8 0.7 %copy-start.2 = (s32[128]{0:T(128)S(1)}, s32[128]{0:T(128)}, u32[]{:S(2)}) copy-start(s32[128]{0:T(128)} %param.4) | copy-start | bytes 1540

commit v4 on v3

--- a/solution.py
+++ b/solution.py
@@ -32,9 +32,9 @@
     return jnp.dot(a, b, preferred_element_type=F32)
 
 
-def kernel(n_ta, n_ch, rows, length, n_parts, raw_ref, band_hbm, taps_hbm, out_ref,
-           band_ref, taps_ref, x, xe, f, pre, suf, nbuf, own, shifted, qbuf, pt, acc, w_hi, w_lo, tri, xs_hi, xs_lo,
-           small_sem, local_sem, raw_send, raw_recv, z_send, q_recv, y_send, out_sem):
+def kernel(n_ta, n_ch, rows, length, n_parts, raw_ref, band_hbm, taps_hbm, acc,
+           band_ref, taps_ref, x, xe, f, pre, suf, nbuf, own, shifted, qbuf, pt, w_hi, w_lo, tri, xs_hi, xs_lo,
+           small_sem, local_sem, raw_send, raw_recv, z_send, q_recv, y_send):
     a = lax.axis_index("ta")
     c = lax.axis_index("ch")
     off = n_ch // 4
@@ -146,6 +146,10 @@
                     picked = jnp.where(bands == float(b), one[:, b * 128:(b + 1) * 128], picked)
                 f[:, 128 * (4 * m + q):128 * (4 * m + q + 1)] = picked
 
+        pending = [k for k in range(n_chunks) if h > 0]
+        for k in pending[:n_chunks // 4]:
+            forward(0, k, h - 1)
+
         n_sum = length // 256
         total = jnp.zeros((tall, 1), F32)
         totals = []
@@ -164,6 +168,9 @@
             if m < n_sum - 1:
                 behind = behind + totals[m + 1]
                 suf[:, lanes] = suf[:, lanes] + behind
+
+        for k in pending[n_chunks // 4:n_chunks // 2]:
+            forward(0, k, h - 1)
 
         ours = slice(h * hr, (h + 1) * hr)
         for k in range(n_chunks):
@@ -187,6 +194,8 @@
                 device_id=(up, a), device_id_type=MESH)
             copy.start()
             z_copies.append(copy)
+        for k in pending[n_chunks // 2:]:
+            forward(0, k, h - 1)
 
     step = min(rows, 16)
     n_shift = rows // step
@@ -247,32 +256,18 @@
                     part = acc[where] + part
                 acc[where] = part * scale if last else part
 
-        def send(lag0, n_lags, slot):
-            return pltpu.make_async_copy(
-                acc.at[:, pl.ds(lag0, n_lags)], out_ref.at[:, pl.ds(lag0, n_lags)], out_sem.at[slot])
-
         def body(i, carry):
             b, h = i // 2, i % 2
             piece(i * half, half, pl.multiple_of(h * (half * rows), half * rows),
                   pl.multiple_of(b * FINE, FINE))
-            if last:
-                send(i * half, half, i).start()
             return carry
 
         lax.fori_loop(0, 2 * coarse, body, 0)
         piece(coarse * FINE, 1, 0, coarse * FINE)
-        if last:
-            send(coarse * FINE, 1, 2 * coarse).start()
-            for i in range(2 * coarse):
-                send(i * half, half, i).wait()
-            send(coarse * FINE, 1, 2 * coarse).wait()
 
     for h in range(n_parts):
         prepare(h)
     tail = n_parts - 1
-    for h in range(tail):
-        for k in range(n_chunks):
-            forward(0, k, h)
     early = n_shift // 2
     for i in range(early):
         shift_part(i)
@@ -310,7 +305,7 @@
             pl.BlockSpec(memory_space=pltpu.HBM),
             pl.BlockSpec(memory_space=pltpu.HBM),
         ],
-        out_specs=pl.BlockSpec(memory_space=pl.ANY),
+        out_specs=pl.BlockSpec(memory_space=pltpu.VMEM),
         scratch_shapes=[
             pltpu.VMEM((1, block), jnp.int32),
             pltpu.SMEM((NBANDS, TAPS), F32),
@@ -324,7 +319,6 @@
             pltpu.VMEM((FINE * rows, whole + PADK), BF16),
             pltpu.VMEM((ROUNDS, n_chunks, block, chunk), BF16),
             pltpu.VMEM((2 * LAGH + whole + PADK, ROUNDS * block), BF16),
-            pltpu.VMEM((ROUNDS, LAGS, rows, block), F32),
             pltpu.VMEM((256, NBANDS * 128), BF16),
             pltpu.VMEM((256, NBANDS * 128), BF16),
             pltpu.VMEM((256, 512), BF16),
@@ -337,7 +331,6 @@
             dma((ROUNDS, n_chunks, n_parts)),
             dma((ROUNDS, n_chunks, n_parts, n_ta)),
             dma((ROUNDS, n_chunks, n_parts, n_ta)),
-            dma((2 * (LAGS // FINE) + 1,)),
         ],
         compiler_params=pltpu.CompilerParams(
             collective_id=0, has_side_effects=True, vmem_limit_bytes=32 * 1024 * 1024),

time: 52.9 us -> 52.4 us (level)
  no operation moved by 1% of the time
where the time goes in v4:
time: 52.4 us; the launch traced here: 52.2 us
  Pallas kernels  47.7 us (91%)
  local copies, waits for them, and re-layouts  4.51 us (9%)
    pallas_call x1, Pallas kernels, on_device(): pl.pallas_call(functools.partial(kernel, n_ta, n_ch, rows, length, n_part...  47.7 us
    unnamed x7, local copies, waits for them, and re-layouts  4.51 us

profile of v4, /device:TPU:0, one launch (start us, length us, event | category | flops | bytes accessed | tf_op | source)
XLA Modules:
  0.0 52.2 jit_solution(17375958684115375826)
XLA Ops:
  0.0 0.0 copy-start
  0.0 1.1 %copy-done = f32[128,1536]{1,0:T(8,128)S(1)} copy-done((f32[128,1536]{1,0:T(8,128)S(1)}, f32[128,1536]{1,0:T(8,128)}, u32[]{:S(2)}) %copy-start) | copy-done | bytes 786456
  1.1 0.0 copy-start.1
  1.1 0.7 %copy-done.1 = f32[4,33]{1,0:T(4,128)S(1)} copy-done((f32[4,33]{1,0:T(4,128)S(1)}, f32[4,33]{1,0:T(4,128)}, u32[]{:S(2)}) %copy-start.1) | copy-done | bytes 552
  1.8 0.0 copy-start.2
  1.8 0.7 %copy-done.2 = s32[128]{0:T(128)S(1)} copy-done((s32[128]{0:T(128)S(1)}, s32[128]{0:T(128)}, u32[]{:S(2)}) %copy-start.2) | copy-done | bytes 536
  2.5 47.7 %shard_map.37 = f32[2,65,64,128]{3,2,1,0:T(8,128)S(1)} custom-call(f32[128,1536]{1,0:T(8,128)S(1)} %copy-done, s32[1,128]{1,0:T(1,128)S(1)} %bitcast.1, f32[4,33]{1,0:T(4,128)S(1)} %copy-done.1), custom_call_target="tpu_custom_call" | custom-call | tf_op jit(solution)/shard_map/pallas_call | solution.py:300
  50.1 2.0 %copy.5 = f32[2,65,64,128]{3,2,1,0:T(8,128)} copy(f32[2,65,64,128]{3,2,1,0:T(8,128)S(1)} %shard_map.37) | data formatting | bytes 8519680
Async XLA Ops:
  0.0 1.1 %copy-start = (f32[128,1536]{1,0:T(8,128)S(1)}, f32[128,1536]{1,0:T(8,128)}, u32[]{:S(2)}) copy-start(f32[128,1536]{1,0:T(8,128)} %raw_ref.1) | copy-start | bytes 2359300
  1.1 0.7 %copy-start.1 = (f32[4,33]{1,0:T(4,128)S(1)}, f32[4,33]{1,0:T(4,128)}, u32[]{:S(2)}) copy-start(f32[4,33]{1,0:T(4,128)} %taps_hbm.1) | copy-start | bytes 1588
  1.8 0.7 %copy-start.2 = (s32[128]{0:T(128)S(1)}, s32[128]{0:T(128)}, u32[]{:S(2)}) copy-start(s32[128]{0:T(128)} %param.4) | copy-start | bytes 1540

commit v5 on v4

--- a/solution.py
+++ b/solution.py
@@ -15,7 +15,7 @@
 LAGS = 65
 ROUNDS = 2
 FINE = 16
-SUBS = 2
+SUBS = 3
 PARTS = 2
 PADK = 128
 MESH = pl.DeviceIdType.MESH

time: 52.4 us -> 56.8 us (1.084)
  Pallas kernels: 47.7 us -> 52.1 us
    pallas_call x1, Pallas kernels: 47.7 us -> 52.1 us  [on_device(): pl.pallas_call(functools.partial(kernel, n_ta, n_ch, rows, length, n_part...]
where the time goes in v5:
time: 56.8 us; the launch traced here: 56.7 us
  Pallas kernels  52.1 us (92%)
  local copies, waits for them, and re-layouts  4.51 us (8%)
    pallas_call x1, Pallas kernels, on_device(): pl.pallas_call(functools.partial(kernel, n_ta, n_ch, rows, length, n_part...  52.1 us
    unnamed x7, local copies, waits for them, and re-layouts  4.51 us

profile of v5, /device:TPU:0, one launch (start us, length us, event | category | flops | bytes accessed | tf_op | source)
XLA Modules:
  0.0 56.7 jit_solution(686454959473625537)
XLA Ops:
  0.0 0.0 copy-start
  0.0 1.1 %copy-done = f32[128,1536]{1,0:T(8,128)S(1)} copy-done((f32[128,1536]{1,0:T(8,128)S(1)}, f32[128,1536]{1,0:T(8,128)}, u32[]{:S(2)}) %copy-start) | copy-done | bytes 786456
  1.1 0.0 copy-start.1
  1.1 0.7 %copy-done.1 = f32[4,33]{1,0:T(4,128)S(1)} copy-done((f32[4,33]{1,0:T(4,128)S(1)}, f32[4,33]{1,0:T(4,128)}, u32[]{:S(2)}) %copy-start.1) | copy-done | bytes 552
  1.8 0.0 copy-start.2
  1.8 0.7 %copy-done.2 = s32[128]{0:T(128)S(1)} copy-done((s32[128]{0:T(128)S(1)}, s32[128]{0:T(128)}, u32[]{:S(2)}) %copy-start.2) | copy-done | bytes 536
  2.5 52.1 %shard_map.37 = f32[2,65,64,128]{3,2,1,0:T(8,128)S(1)} custom-call(f32[128,1536]{1,0:T(8,128)S(1)} %copy-done, s32[1,128]{1,0:T(1,128)S(1)} %bitcast.1, f32[4,33]{1,0:T(4,128)S(1)} %copy-done.1), custom_call_target="tpu_custom_call" | custom-call | tf_op jit(solution)/shard_map/pallas_call | solution.py:300
  54.6 2.0 %copy.5 = f32[2,65,64,128]{3,2,1,0:T(8,128)} copy(f32[2,65,64,128]{3,2,1,0:T(8,128)S(1)} %shard_map.37) | data formatting | bytes 8519680
Async XLA Ops:
  0.0 1.1 %copy-start = (f32[128,1536]{1,0:T(8,128)S(1)}, f32[128,1536]{1,0:T(8,128)}, u32[]{:S(2)}) copy-start(f32[128,1536]{1,0:T(8,128)} %raw_ref.1) | copy-start | bytes 2359300
  1.1 0.7 %copy-start.1 = (f32[4,33]{1,0:T(4,128)S(1)}, f32[4,33]{1,0:T(4,128)}, u32[]{:S(2)}) copy-start(f32[4,33]{1,0:T(4,128)} %taps_hbm.1) | copy-start | bytes 1588
  1.8 0.7 %copy-start.2 = (s32[128]{0:T(128)S(1)}, s32[128]{0:T(128)}, u32[]{:S(2)}) copy-start(s32[128]{0:T(128)} %param.4) | copy-start | bytes 1540
